TPU v7x, 512 devices: a whole 4x4x16 slice. The times are simulated.
512 devices in a mesh: row: 128 (over z, y, core), col: 4 (over x).
Axes of the slice: x: 4, y: 4, z: 16, core: 2. Of those that a mesh axis runs over, the one named last changes fastest.
Arguments:
- travel_times: bfloat16 [131072, 8192], P('row', 'col'), may hold values from -18 to 18, as said below
- test_matrix: bfloat16 [8192, 512], P(('col', 'row')), may hold values from -0.198873782 to 0.198873782, as said below
Outputs:
- basis: float32 [131072, 512], P(('row', 'col'))
- factor: float32 [512, 512], P('col')
Inputs may be any that keep to these rules, and one draw needn't show every extreme that they name: `travel_times`: finite values. `test_matrix`: finite values.
All inputs are finite; a program needn't handle non-finite values.
Results may differ from a plain program's by a relative error of at most 0.0003.
Values may be sent and summed in bfloat16 or wider, within the bound.
A program may use at most 64 MiB of HBM per device.

v0:
```python
import jax
import jax.numpy as jnp
from jax import lax
from jax.sharding import PartitionSpec as P


def on_device(travel_times, test_matrix):
    rows_here = travel_times.shape[0]
    sketch_width = test_matrix.shape[1]
    groups = lax.axis_size("col")
    share_rows = rows_here // groups
    partial_sketch = jnp.dot(
        travel_times,
        lax.all_gather(test_matrix, "row", axis=0, tiled=True),
        preferred_element_type=jnp.float32,
    )
    summed = lax.psum(partial_sketch, "col")
    sketch = lax.dynamic_slice_in_dim(summed, lax.axis_index("col") * share_rows, share_rows, 0)
    total_rows = rows_here * lax.axis_size("row")
    gram_local = jnp.dot(
        sketch.T, sketch, precision=lax.Precision.HIGHEST, preferred_element_type=jnp.float32
    )
    gram_mean = lax.psum(gram_local, ("row", "col")) / total_rows
    lower_factor = jnp.linalg.cholesky(gram_mean)
    basis_rows = jax.scipy.linalg.solve_triangular(lower_factor, sketch.T, lower=True).T
    factor_width = sketch_width // groups
    factor_rows = lax.dynamic_slice_in_dim(
        lower_factor.T, lax.axis_index("col") * factor_width, factor_width, 0
    )
    return (basis_rows, factor_rows)


def solution(mesh):
    placed = (P("row", "col"), P(("col", "row"), None))
    return jax.shard_map(
        on_device,
        mesh=mesh,
        in_specs=placed,
        out_specs=(P(("row", "col"), None), P("col", None)),
        check_vma=False,
    )
```

profile of v0, /device:TPU:1, one launch (start us, length us, event | category | flops | bytes accessed | tf_op | source)
XLA Modules:
  0.0 853.2 jit_solution(10997507328910923579)
XLA Ops:
  7.9 148.8 %all-gather.2.cloned.1.call-done = bf16[2048,512]{1,0:T(8,128)(2,1)} async-done(((bf16[16,512]{1,0:T(8,128)(2,1)}), bf16[2048,512]{1,0:T(8,128)(2,1)}) %all-gather.2.cloned.1.call-update) | async-done | bytes 2097168 | tf_op jit(solution)/shard_map/all_gather | solution.py:14
  156.7 6.5 fusion.35
  163.3 69.9 %all-reduce.4.cloned.1.call-done = f32[1024,512]{1,0:T(8,128)} async-done(((f32[1024,512]{1,0:T(8,128)}), f32[1024,512]{1,0:T(8,128)}) %all-reduce.4.cloned.1.call-update) | async-done | bytes 2097168 | tf_op jit(solution)/shard_map/psum | solution.py:17
  233.2 3.2 fusion.2
  236.5 1.9 dynamic-slice_bitcast_fusion
  238.4 468.2 %all-reduce.6.cloned.1.call-done = f32[512,512]{0,1:T(8,128)} async-done(((f32[512,512]{0,1:T(8,128)}), f32[512,512]{0,1:T(8,128)}) %all-reduce.6.cloned.1.call-update) | async-done | bytes 1048592 | tf_op jit(solution)/shard_map/psum | solution.py:23
  706.6 1.4 broadcast_multiply_fusion
  708.6 11.7 %cholesky.104 = f32[128,128]{1,0:T(8,128)S(1)} custom-call(f32[128,128]{1,0:T(8,128)S(1)} %cholesky.266), custom_call_target="Cholesky" | custom-call | tf_op jit(solution)/shard_map/jit(cholesky)/cholesky | solution.py:24
  720.5 9.8 %custom-call.31 = f32[1,128,128]{1,2,0:T(8,128)S(1)} custom-call(f32[1,128,128]{2,1,0:T(8,128)S(1)} %get-tuple-element.33), custom_call_target="InvertDiagBlocksLowerTriangular" | custom-call | tf_op jit(solution)/shard_map/jit(cholesky)/cholesky | solution.py:24
  731.0 11.8 %cholesky.217 = f32[128,128]{1,0:T(8,128)S(1)} custom-call(f32[128,128]{1,0:T(8,128)S(1)} %cholesky.270), custom_call_target="Cholesky" | custom-call | tf_op jit(solution)/shard_map/jit(cholesky)/cholesky | solution.py:24
  742.8 9.8 %custom-call.32 = f32[1,128,128]{1,2,0:T(8,128)S(1)} custom-call(f32[1,128,128]{2,1,0:T(8,128)S(1)} %get-tuple-element.30), custom_call_target="InvertDiagBlocksLowerTriangular" | custom-call | tf_op jit(solution)/shard_map/jit(cholesky)/cholesky | solution.py:24
  753.3 11.7 %cholesky.238 = f32[128,128]{1,0:T(8,128)S(1)} custom-call(f32[128,128]{1,0:T(8,128)S(1)} %cholesky.275), custom_call_target="Cholesky" | custom-call | tf_op jit(solution)/shard_map/jit(cholesky)/cholesky | solution.py:24
  765.0 9.8 %custom-call.33 = f32[1,128,128]{1,2,0:T(8,128)S(1)} custom-call(f32[1,128,128]{2,1,0:T(8,128)S(1)} %get-tuple-element.27), custom_call_target="InvertDiagBlocksLowerTriangular" | custom-call | tf_op jit(solution)/shard_map/jit(cholesky)/cholesky | solution.py:24
  775.5 11.9 %cholesky.255 = f32[128,128]{1,0:T(8,128)S(1)} custom-call(f32[128,128]{1,0:T(8,128)S(1)} %convolution_subtract_fusion.5), custom_call_target="Cholesky" | custom-call | tf_op jit(solution)/shard_map/jit(cholesky)/cholesky | solution.py:24
  792.0 1.3 fusion.1
  793.3 8.1 while.1
  793.9 1.3 bitcast_dynamic-update-slice_fusion.2
  796.0 1.3 bitcast_dynamic-update-slice_fusion.2
  798.0 1.3 bitcast_dynamic-update-slice_fusion.2
  800.0 1.3 bitcast_dynamic-update-slice_fusion.2
  801.4 39.3 %custom-call.34 = f32[4,128,128]{1,2,0:T(8,128)S(1)} custom-call(f32[4,128,128]{2,1,0:T(8,128)S(1)} %get-tuple-element.9), custom_call_target="InvertDiagBlocksLowerTriangular" | custom-call | tf_op jit(solution)/shard_map/jit(_solve_triangular)/triangular_solve | solution.py:25
  843.9 1.0 copy.6
  844.8 1.0 dynamic-slice_bitcast_fusion.1
  845.8 0.8 copy.7
  (48 shorter events, 11.4 us)
Async XLA Ops:
  7.2 149.6 %all-gather.2.cloned.1.call-start = ((), (), s32[]{:S(2)}) async-start(), calls=%async_computation | async-start | bytes 2113536 | tf_op jit(solution)/shard_map/all_gather | solution.py:14
  7.9 225.3 %all-reduce.4.cloned.1.call-start = ((), (), s32[]{:S(2)}) async-start(), calls=%async_computation.1 | async-start | bytes 4194304 | tf_op jit(solution)/shard_map/psum | solution.py:17
  163.2 543.3 %all-reduce.6.cloned.1.call-start = ((), (), s32[]{:S(2)}) async-start(), calls=%async_computation.2 | async-start | bytes 2097152 | tf_op jit(solution)/shard_map/psum | solution.py:23
  706.6 1.8 copy-start
  775.5 65.3 %copy-start.1 = (f32[512,256]{0,1:T(8,128)S(1)}, f32[512,256]{0,1:T(8,128)}, u32[]{:S(2)}) copy-start(f32[512,256]{0,1:T(8,128)} %dynamic-slice_bitcast_fusion) | copy-start | bytes 1572868
Sparse Core Ops, SparseCore 0:
  11.1 145.5 all-gather.1
  163.4 69.8 all-reduce.3
  239.6 466.9 all-reduce.5
where the time goes:
time: 854 us; the launch traced here: 853 us
  waiting for transfers between devices  688 us (81%)
  other arithmetic  121 us (14%)
  between operations  16.5 us (2%)
  matrix products  14.6 us (2%)
  local copies, waits for them, and re-layouts  13.2 us (2%)
    psum x1, waiting for transfers between devices, on_device(): gram_mean = lax.psum(gram_local, ('row', 'col')) / total_rows  468 us
    all_gather x1, waiting for transfers between devices, on_device(): lax.all_gather(test_matrix, 'row', axis=0, tiled=True)  149 us
    another operation x14, other arithmetic, on_device(): lower_factor = jnp.linalg.cholesky(gram_mean)  78.8 us
    psum x1, waiting for transfers between devices, on_device(): summed = lax.psum(partial_sketch, 'col')  69.9 us
    another operation x3, other arithmetic, on_device(): jax.scipy.linalg.solve_triangular(lower_factor, sketch.T, lower=True)  40.6 us
  transfers between devices with their start and end apart: 3, of which 3 were waited for; matrix products, arithmetic and copies ran while one was open for 0% of the time, Pallas kernels for 0%

commit v1 on v0

v1 whole, which is shorter than its diff:
```python
import functools
import jax
import jax.numpy as jnp
from jax import lax
from jax.experimental import pallas as pl
from jax.experimental.pallas import tpu as pltpu
from jax.sharding import PartitionSpec as P

NY = 4
NC = 2
W = 128
CHUNKS = 4
MESH = pl.DeviceIdType.MESH


def comm_kernel(nz, nx, a_hbm, t_ref, s_ref, fin, a_v, tg, part, rsr, own, crecv, hb, prs, zr, a_sem, zs, ys, ks, rs, cs, ps, gz, ag, ck):
    ny = NY
    r = lax.axis_index("row")
    x = lax.axis_index("col")
    c = lax.rem(r, NC)
    y = lax.rem(r // NC, ny)
    z = r // (NC * ny)
    ns = ny * nx
    s = y * nx + x
    share = s_ref.shape[0]

    def row_of(zz, yy, cc):
        return (zz * ny + yy) * NC + cc

    def z_peer(i):
        return (row_of(lax.rem(z + i, nz), y, c), x)

    def plane_peer(i):
        q = lax.rem(s + i, ns)
        return q, (row_of(z, q // nx, c), lax.rem(q, nx))

    sibling = (row_of(z, y, 1 - c), x)

    load_a = pltpu.make_async_copy(a_hbm, a_v, a_sem)
    load_a.start()
    barrier = pltpu.get_barrier_semaphore()

    def greet_z(i, carry):
        pl.semaphore_signal(barrier, inc=1, device_id=z_peer(i), device_id_type=MESH)
        return carry

    def greet_plane(i, carry):
        pl.semaphore_signal(barrier, inc=1, device_id=plane_peer(i)[1], device_id_type=MESH)
        return carry

    lax.fori_loop(1, nz, greet_z, 0)
    lax.fori_loop(1, ns, greet_plane, 0)
    pl.semaphore_signal(barrier, inc=1, device_id=sibling, device_id_type=MESH)
    for j in range(CHUNKS):
        tg[j, z, y, c] = t_ref[:, j * W : (j + 1) * W]
    pl.semaphore_wait(barrier, nz + ns - 1)

    def rcopy(src, dst, sems, k, to):
        return pltpu.make_async_remote_copy(
            src_ref=src, dst_ref=dst, send_sem=sems.at[0, k], recv_sem=sems.at[1, k],
            device_id=to, device_id_type=MESH,
        )

    def wait_bytes(view, sem):
        pltpu.make_async_copy(view, view, sem).wait()

    def z_send(j):
        def body(i, carry):
            rcopy(t_ref.at[:, pl.ds(j * W, W)], tg.at[j, z, y, c], zs, j, z_peer(i)).start()
            return carry
        lax.fori_loop(1, nz, body, 0)

    def z_view(j):
        return tg.at[j, pl.ds(0, nz - 1), y, c]

    def y_send(j):
        def body(i, carry):
            rcopy(tg.at[j, :, y, c], tg.at[j, :, y, c], ys, j, (row_of(z, lax.rem(y + i, ny), c), x)).start()
            return carry
        lax.fori_loop(1, ny, body, 0)

    def y_view(j):
        return tg.at[j, :, pl.ds(0, ny - 1), c]

    def k_copy(j):
        return rcopy(tg.at[j, :, :, c], tg.at[j, :, :, c], ks, j, sibling)

    def project(j):
        t_all = tg[j].reshape(-1, W)

        def block(d):
            q = lax.rem(x + d, nx)
            rows = pl.ds(pl.multiple_of(q * share, share), share)
            return q, jnp.dot(a_v[rows, :], t_all, preferred_element_type=jnp.float32)

        def body(i, carry):
            d = nx - 1 - i
            q, value = block(d)
            part[j, d] = value
            rcopy(part.at[j, d], rsr.at[j, d - 1], rs, j, (r, q)).start()
            return carry
        lax.fori_loop(0, nx - 1, body, 0)
        part[j, 0] = block(0)[1]

    def rs_view(j):
        return rsr.at[j]

    def finish_chunk(j):
        wait_bytes(rs_view(j), rs.at[1, j])
        total = part[j, 0]
        for d in range(nx - 1):
            total = total + rsr[j, d]
        s_ref[:, j * W : (j + 1) * W] = total

    def gram_block(i, j):
        return lax.dot_general(
            s_ref[:, i * W : (i + 1) * W], s_ref[:, j * W : (j + 1) * W], (((0,), (0,)), ((), ())),
            precision=lax.Precision.HIGHEST, preferred_element_type=jnp.float32,
        )

    places = {
        0: [[(0, 0), (0, 1)], [(1, 0), (1, 1)]],
        1: [[(2, 0), (2, 1)], [(2, 2), None]],
        2: [[(3, 0), (3, 1)], [(3, 2), (3, 3)]],
    }

    def gram(g):
        for half in range(2):
            for k in range(2):
                place = places[g][half][k]
                own[g, half, :, k * W : (k + 1) * W] = jnp.zeros((W, W), jnp.float32) if place is None else gram_block(*place)
        rcopy(own.at[g, 1 - c], crecv.at[g], cs, g, sibling).start()

    def plane_send(g):
        wait_bytes(crecv.at[g], cs.at[1, g])
        hb[g] = (own[g, c] + crecv[g]).reshape(hb.shape[1:])

        def body(i, carry):
            q, to = plane_peer(i)
            rcopy(hb.at[g, q], prs.at[g, s], ps, g, to).start()
            return carry
        lax.fori_loop(1, ns, body, 0)
        prs[g, s] = hb[g, s]

    def plane_view(g):
        return prs.at[g, pl.ds(0, ns - 1)]

    def z_gram_send(g):
        wait_bytes(plane_view(g), ps.at[1, g])
        zr[g, z] = jnp.sum(prs[g], axis=0)

        def body(i, carry):
            rcopy(zr.at[g, z], zr.at[g, z], gz, g, z_peer(i)).start()
            return carry
        lax.fori_loop(1, nz, body, 0)

    def z_gram_view(g):
        return zr.at[g, pl.ds(0, nz - 1)]

    def spread(g):
        wait_bytes(z_gram_view(g), gz.at[1, g])
        fin[g, c, s] = jnp.sum(zr[g], axis=0)

        def body(i, carry):
            rcopy(fin.at[g, c, s], fin.at[g, c, s], ag, g, plane_peer(i)[1]).start()
            return carry
        lax.fori_loop(1, ns, body, 0)

    def spread_view(g):
        return fin.at[g, c, pl.ds(0, ns - 1)]

    def spread_core(g):
        wait_bytes(spread_view(g), ag.at[1, g])
        rcopy(fin.at[g, c], fin.at[g, c], ck, g, sibling).start()

    def spread_end(g):
        wait_bytes(fin.at[g, c], ck.at[1, g])

    for j in range(CHUNKS):
        z_send(j)

    def do_z(j):
        wait_bytes(z_view(j), zs.at[1, j])
        y_send(j)

    def do_y(j):
        wait_bytes(y_view(j), ys.at[1, j])
        k_copy(j).start()

    def do_k(j):
        wait_bytes(tg.at[j, :, :, c], ks.at[1, j])
        project(j)

    do_z(0)
    do_z(1)
    do_z(2)
    do_y(0)
    do_z(3)
    load_a.wait()
    do_k(0)
    do_y(1)
    do_k(1)
    do_y(2)
    do_k(2)
    do_y(3)
    do_k(3)
    finish_chunk(0)
    finish_chunk(1)
    gram(0)
    plane_send(0)
    finish_chunk(2)
    gram(1)
    plane_send(1)
    z_gram_send(0)
    finish_chunk(3)
    gram(2)
    plane_send(2)
    z_gram_send(1)
    z_gram_send(2)
    for g in range(3):
        spread(g)
        if g:
            spread_core(g - 1)
    spread_core(2)
    for g in range(3):
        spread_end(g)

    for j in range(CHUNKS):
        wait_bytes(z_view(j), zs.at[0, j])
        wait_bytes(y_view(j), ys.at[0, j])
        wait_bytes(tg.at[j, :, :, c], ks.at[0, j])
        wait_bytes(rs_view(j), rs.at[0, j])
    for g in range(3):
        wait_bytes(crecv.at[g], cs.at[0, g])
        wait_bytes(plane_view(g), ps.at[0, g])
        wait_bytes(z_gram_view(g), gz.at[0, g])
        wait_bytes(spread_view(g), ag.at[0, g])
        wait_bytes(fin.at[g, c], ck.at[0, g])


def communicate(mesh, travel_times, test_matrix):
    nx = mesh.shape["col"]
    nz = mesh.shape["row"] // (NY * NC)
    rows, cols = travel_times.shape
    depth = test_matrix.shape[0]
    share = rows // nx
    ns = NY * nx
    pr = W // ns
    f32 = jnp.float32
    dma = pltpu.SemaphoreType.DMA
    return pl.pallas_call(
        functools.partial(comm_kernel, nz, nx),
        out_shape=(
            jax.ShapeDtypeStruct((share, CHUNKS * W), f32),
            jax.ShapeDtypeStruct((3, 2, ns, pr, 2 * W), f32),
        ),
        in_specs=[pl.BlockSpec(memory_space=pl.ANY), pl.BlockSpec(memory_space=pltpu.VMEM)],
        out_specs=[pl.BlockSpec(memory_space=pltpu.VMEM)] * 2,
        scratch_shapes=[
            pltpu.VMEM((rows, cols), jnp.bfloat16),
            pltpu.VMEM((CHUNKS, nz, NY, NC, depth, W), jnp.bfloat16),
            pltpu.VMEM((CHUNKS, nx, share, W), f32),
            pltpu.VMEM((CHUNKS, nx - 1, share, W), f32),
            pltpu.VMEM((3, 2, W, 2 * W), f32),
            pltpu.VMEM((3, W, 2 * W), f32),
            pltpu.VMEM((3, ns, pr, 2 * W), f32),
            pltpu.VMEM((3, ns, pr, 2 * W), f32),
            pltpu.VMEM((3, nz, pr, 2 * W), f32),
            dma,
        ]
        + [dma((2, CHUNKS))] * 4
        + [dma((2, 3))] * 5,
        compiler_params=pltpu.CompilerParams(
            collective_id=0, has_side_effects=True, vmem_limit_bytes=40 << 20
        ),
    )(travel_times, test_matrix)


def gram_of(fin):
    halves = fin.reshape(3, 2, W, 2 * W)
    zero = jnp.zeros((W, W), jnp.float32)
    low = jnp.concatenate([
        jnp.concatenate([halves[0, 0], zero, zero], 1),
        jnp.concatenate([halves[0, 1], zero, zero], 1),
        jnp.concatenate([halves[1, 0], halves[1, 1]], 1),
        jnp.concatenate([halves[2, 0], halves[2, 1]], 1),
    ], 0)
    return low


def solution(mesh):
    def on_device(travel_times, test_matrix):
        sketch, fin = communicate(mesh, travel_times, test_matrix)
        total_rows = travel_times.shape[0] * mesh.shape["row"]
        gram_mean = gram_of(fin) / total_rows
        lower = lax.linalg.cholesky(gram_mean, symmetrize_input=False)
        basis = jax.scipy.linalg.solve_triangular(lower, sketch.T, lower=True).T
        width = lower.shape[0] // mesh.shape["col"]
        rows = lax.dynamic_slice_in_dim(lower.T, lax.axis_index("col") * width, width, 0)
        return basis, rows

    return jax.shard_map(
        on_device, mesh=mesh, in_specs=(P("row", "col"), P(("col", "row"), None)),
        out_specs=(P(("row", "col"), None), P("col", None)), check_vma=False,
    )
```

time: 854 us -> 235 us (0.28)
  waiting for transfers between devices: 688 us -> 0 us
  Pallas kernels: 0 us -> 92.4 us
  between operations: 16.5 us -> 3.44 us
  matrix products: 14.6 us -> 4.91 us
    psum x2 -> x0, waiting for transfers between devices: 538 us -> none  [the longest x1 468 us: on_device(): gram_mean = lax.psum(gram_local, ('row', 'col')) / total_rows]
    all_gather x1 -> x0, waiting for transfers between devices: 149 us -> none  [on_device(): lax.all_gather(test_matrix, 'row', axis=0, tiled=True)]
    pallas_call x0 -> x1, Pallas kernels: none -> 92.4 us  [communicate(): pl.pallas_call(functools.partial(comm_kernel, nz, nx), out_shape=(jax.Sha...]
    dot_general x2 -> x0, matrix products: 9.72 us -> none  [the longest x1 6.48 us: on_device(): jnp.dot(travel_times, lax.all_gather(test_matrix, 'row', axis=0, tiled=Tr...]
  transfers between devices with their start and end apart: 3 -> 0, of which waited for: 3 -> 0; matrix products, arithmetic and copies ran while one was open for 0% -> 0% of each run, Pallas kernels for 0% -> 0%
where the time goes in v1:
time: 235 us
  other arithmetic  120 us (51%)
  Pallas kernels  92.4 us (39%)
  local copies, waits for them, and re-layouts  14.3 us (6%)
  matrix products  4.91 us (2%)
  between operations  3.44 us (1%)
    pallas_call x1, Pallas kernels, communicate(): pl.pallas_call(functools.partial(comm_kernel, nz, nx), out_shape=(jax.Sha...  92.4 us
    another operation x14, other arithmetic, on_device(): lower = lax.linalg.cholesky(gram_mean, symmetrize_input=False)  78.5 us
    another operation x3, other arithmetic, on_device(): basis = jax.scipy.linalg.solve_triangular(lower, sketch.T, lower=True).T  40.8 us
    another operation x12, local copies, waits for them, and re-layouts  8.39 us
    unnamed x6, local copies, waits for them, and re-layouts  4.73 us

profile of v1, /device:TPU:1, one launch (start us, length us, event | category | flops | bytes accessed | tf_op | source)
XLA Modules:
  0.0 234.7 jit_solution(5284636056329063403)
XLA Ops:
  0.6 2.2 copy-done
  2.8 0.7 copy-done.1
  3.5 92.4 %shard_map.41 = (f32[256,512]{1,0:T(8,128)S(1)}, f32[3,2,16,8,256]{4,3,2,1,0:T(8,128)S(1)}) custom-call(bf16[1024,2048]{1,0:T(8,128)(2,1)S(1)} %copy-done, bf16[16,512]{1,0:T(8,128)(2,1)S(1)} %copy-done.1), custom_call_target="tpu_custom_call" | custom-call | tf_op jit(solution)/shard_map/pallas_call | solution.py:251
  96.2 11.7 %cholesky.104 = f32[128,128]{1,0:T(8,128)S(1)} custom-call(f32[128,128]{1,0:T(8,128)S(1)} %cholesky.266), custom_call_target="Cholesky" | custom-call | tf_op jit(solution)/shard_map/cholesky | solution.py:296
  107.9 9.8 %custom-call.24 = f32[1,128,128]{1,2,0:T(8,128)S(1)} custom-call(f32[1,128,128]{2,1,0:T(8,128)S(1)} %get-tuple-element.43), custom_call_target="InvertDiagBlocksLowerTriangular" | custom-call | tf_op jit(solution)/shard_map/cholesky | solution.py:296
  118.6 11.7 %cholesky.217 = f32[128,128]{1,0:T(8,128)S(1)} custom-call(f32[128,128]{1,0:T(8,128)S(1)} %cholesky.270), custom_call_target="Cholesky" | custom-call | tf_op jit(solution)/shard_map/cholesky | solution.py:296
  130.3 0.6 compare_reduce_fusion.2
  132.3 10.0 %custom-call.25 = f32[1,128,128]{1,2,0:T(8,128)S(1)} custom-call(f32[1,128,128]{2,1,0:T(8,128)S(1)} %get-tuple-element.40), custom_call_target="InvertDiagBlocksLowerTriangular" | custom-call | tf_op jit(solution)/shard_map/cholesky | solution.py:296
  142.9 11.7 %cholesky.238 = f32[128,128]{1,0:T(8,128)S(1)} custom-call(f32[128,128]{1,0:T(8,128)S(1)} %cholesky.275), custom_call_target="Cholesky" | custom-call | tf_op jit(solution)/shard_map/cholesky | solution.py:296
  154.7 0.6 compare_reduce_fusion.1
  156.0 9.8 %custom-call.26 = f32[1,128,128]{1,2,0:T(8,128)S(1)} custom-call(f32[1,128,128]{2,1,0:T(8,128)S(1)} %get-tuple-element.37), custom_call_target="InvertDiagBlocksLowerTriangular" | custom-call | tf_op jit(solution)/shard_map/cholesky | solution.py:296
  166.4 11.7 %cholesky.255 = f32[128,128]{1,0:T(8,128)S(1)} custom-call(f32[128,128]{1,0:T(8,128)S(1)} %convolution_subtract_fusion.5), custom_call_target="Cholesky" | custom-call | tf_op jit(solution)/shard_map/cholesky | solution.py:296
  178.1 0.6 compare_reduce_fusion
  179.4 1.3 fusion.3
  180.7 8.5 %while.1 = (s32[]{:T(128)}, f32[512,512]{1,0:T(8,128)S(1)}, s32[4,2]{0,1:T(2,128)S(1)}, f32[4,128,128]{2,1,0:T(8,128)S(1)}, s32[]{:T(128)}) while((s32[]{:T(128)}, f32[512,512]{1,0:T(8,128)S(1)}, s32[4,2]{0,1:T(2,128)S(1)}, f32[4,128,128]{2,1,0:T(8,128)S(1)}, s32[]{:T(128)}) %tuple.38), condition=%wide.while_cond, body=%wide.while_body.sunk | while | flops 2 | bytes 131181 | solution.py:297
  181.4 1.4 bitcast_dynamic-update-slice_fusion.2
  183.5 1.4 bitcast_dynamic-update-slice_fusion.2
  185.6 1.4 bitcast_dynamic-update-slice_fusion.2
  187.7 1.4 bitcast_dynamic-update-slice_fusion.2
  189.2 39.6 %custom-call.27 = f32[4,128,128]{1,2,0:T(8,128)S(1)} custom-call(f32[4,128,128]{2,1,0:T(8,128)S(1)} %get-tuple-element.13), custom_call_target="InvertDiagBlocksLowerTriangular" | custom-call | tf_op jit(solution)/shard_map/jit(_solve_triangular)/triangular_solve | solution.py:297
  230.7 0.8 convolution_subtract_fusion.1
  231.9 1.0 copy.4
  232.9 1.0 dynamic-slice_bitcast_fusion
  233.9 0.8 copy.5
  (36 shorter events, 7.3 us)
Async XLA Ops:
  0.6 2.2 copy-start
  2.8 0.7 copy-start.1

commit v2 on v1

--- a/solution.py
+++ b/solution.py
@@ -276,28 +276,128 @@
     )(travel_times, test_matrix)
 
 
-def gram_of(fin):
-    halves = fin.reshape(3, 2, W, 2 * W)
-    zero = jnp.zeros((W, W), jnp.float32)
-    low = jnp.concatenate([
-        jnp.concatenate([halves[0, 0], zero, zero], 1),
-        jnp.concatenate([halves[0, 1], zero, zero], 1),
-        jnp.concatenate([halves[1, 0], halves[1, 1]], 1),
-        jnp.concatenate([halves[2, 0], halves[2, 1]], 1),
-    ], 0)
-    return low
+HIGHEST = lax.Precision.HIGHEST
+
+
+def mm(a, b, ca, cb):
+    return lax.dot_general(a, b, (((ca,), (cb,)), ((), ())), precision=HIGHEST, preferred_element_type=jnp.float32)
+
+
+def factor_block(w_ref, q_ref):
+    n = W // 8
+    sub = lax.broadcasted_iota(jnp.int32, (8, W), 0)
+    lane = lax.broadcasted_iota(jnp.int32, (8, W), 1)
+
+    def along(v, i):
+        return jnp.broadcast_to(v[:, i : i + 1], (8, W))
+
+    def down(v, i):
+        return jnp.broadcast_to(v[i : i + 1, :], (8, W))
+
+    for t in range(n):
+        q_ref[8 * t : 8 * t + 8, :] = jnp.where(lane == sub + 8 * t, 1.0, 0.0).astype(jnp.float32)
+    for k in range(n):
+        p = w_ref[8 * k : 8 * k + 8, :]
+        q = q_ref[8 * k : 8 * k + 8, :]
+        cols = [along(p, 8 * k + m) for m in range(8)]
+        rinv, below, us, qs = [], [], [], []
+        for m in range(8):
+            ri = lax.rsqrt(down(cols[m], m))
+            l = cols[m] * ri
+            pivots = {}
+            for i in range(m + 1, 8):
+                pivots[i] = down(l, i)
+                cols[i] = cols[i] - l * pivots[i]
+            lm = jnp.where(sub > m, l, 0.0)
+            u = down(p, m) * ri
+            v = down(q, m) * ri
+            p = jnp.where(sub == m, u, p - lm * u)
+            q = jnp.where(sub == m, v, q - lm * v)
+            rinv.append(ri)
+            below.append(pivots)
+            us.append(u)
+            qs.append(v)
+        w_ref[8 * k : 8 * k + 8, :] = p
+        q_ref[8 * k : 8 * k + 8, :] = q
+        for t in range(k + 1, n):
+            wt = w_ref[8 * t : 8 * t + 8, :]
+            qt = q_ref[8 * t : 8 * t + 8, :]
+            ct = [along(wt, 8 * k + m) for m in range(8)]
+            for m in range(8):
+                l = ct[m] * rinv[m]
+                for i in range(m + 1, 8):
+                    ct[i] = ct[i] - l * below[m][i]
+                wt = wt - l * us[m]
+                qt = qt - l * qs[m]
+            w_ref[8 * t : 8 * t + 8, :] = wt
+            q_ref[8 * t : 8 * t + 8, :] = qt
+
+
+def factor_kernel(scale, s_ref, fin, basis_ref, out_ref, upper, low, inv, w_ref, q_ref):
+    nb = CHUNKS
+    row = lax.broadcasted_iota(jnp.int32, (W, W), 0)
+    col = lax.broadcasted_iota(jnp.int32, (W, W), 1)
+
+    def gram(i, j):
+        if i < 2:
+            g, half, k = 0, i, j
+        else:
+            g, half, k = i - 1, j // 2, j % 2
+        return fin[g, half, :, k * W : (k + 1) * W] * scale
+
+    upper[...] = jnp.zeros_like(upper)
+    for b in range(nb):
+        acc = gram(b, b)
+        for m in range(b):
+            acc = acc - mm(low[b, m], low[b, m], 1, 1)
+        w_ref[...] = acc
+        factor_block(w_ref, q_ref)
+        q = q_ref[...]
+        upper[b, :, b * W : (b + 1) * W] = jnp.where(col >= row, w_ref[...], 0.0)
+        inv[b, b] = q
+        for j in range(b + 1, nb):
+            a = gram(j, b)
+            for m in range(b):
+                a = a - mm(low[j, m], low[b, m], 1, 1)
+            a = mm(a, q, 1, 1)
+            low[j, b] = a
+            upper[b, :, j * W : (j + 1) * W] = a.T
+        for j in range(b):
+            total = mm(low[b, j], inv[j, j], 1, 0)
+            for m in range(j + 1, b):
+                total = total + mm(low[b, m], inv[m, j], 1, 0)
+            inv[b, j] = -mm(q, total, 1, 0)
+        value = mm(s_ref[:, 0:W], inv[b, 0], 1, 1)
+        for m in range(1, b + 1):
+            value = value + mm(s_ref[:, m * W : (m + 1) * W], inv[b, m], 1, 1)
+        basis_ref[:, b * W : (b + 1) * W] = value
+    out_ref[...] = upper[lax.axis_index("col")]
+
+
+def finish(scale, sketch, fin):
+    f32 = jnp.float32
+    rows, width = sketch.shape
+    return pl.pallas_call(
+        functools.partial(factor_kernel, scale),
+        out_shape=(jax.ShapeDtypeStruct((rows, width), f32), jax.ShapeDtypeStruct((W, width), f32)),
+        in_specs=[pl.BlockSpec(memory_space=pltpu.VMEM)] * 2,
+        out_specs=[pl.BlockSpec(memory_space=pltpu.VMEM)] * 2,
+        scratch_shapes=[
+            pltpu.VMEM((CHUNKS, W, width), f32),
+            pltpu.VMEM((CHUNKS, CHUNKS, W, W), f32),
+            pltpu.VMEM((CHUNKS, CHUNKS, W, W), f32),
+            pltpu.VMEM((W, W), f32),
+            pltpu.VMEM((W, W), f32),
+        ],
+        compiler_params=pltpu.CompilerParams(vmem_limit_bytes=40 << 20),
+    )(sketch, fin)
 
 
 def solution(mesh):
     def on_device(travel_times, test_matrix):
         sketch, fin = communicate(mesh, travel_times, test_matrix)
         total_rows = travel_times.shape[0] * mesh.shape["row"]
-        gram_mean = gram_of(fin) / total_rows
-        lower = lax.linalg.cholesky(gram_mean, symmetrize_input=False)
-        basis = jax.scipy.linalg.solve_triangular(lower, sketch.T, lower=True).T
-        width = lower.shape[0] // mesh.shape["col"]
-        rows = lax.dynamic_slice_in_dim(lower.T, lax.axis_index("col") * width, width, 0)
-        return basis, rows
+        return finish(1.0 / total_rows, sketch, fin.reshape(3, 2, W, 2 * W))
 
     return jax.shard_map(
         on_device, mesh=mesh, in_specs=(P("row", "col"), P(("col", "row"), None)),

time: 235 us -> 118 us (0.50)
  other arithmetic: 120 us -> 0 us
  Pallas kernels: 92.4 us -> 114 us
  local copies, waits for them, and re-layouts: 14.3 us -> 2.9 us
  matrix products: 4.91 us -> 0 us
  between operations: 3.44 us -> 0.65 us
    another operation x17 -> x0, other arithmetic: 119 us -> none  [the longest x14 78.5 us: on_device(): lower = lax.linalg.cholesky(gram_mean, symmetrize_input=False)]
    pallas_call x0 -> x1, Pallas kernels: none -> 21.3 us  [finish(): pl.pallas_call(functools.partial(factor_kernel, scale), out_shape=(jax.Sh...]
    another operation x17 -> x0, local copies, waits for them, and re-layouts: 8.53 us -> none
    another operation x13 -> x0, matrix products: 4.91 us -> none  [the longest x7 3.03 us: on_device(): basis = jax.scipy.linalg.solve_triangular(lower, sketch.T, lower=True).T]
    unnamed x6 -> x4, local copies, waits for them, and re-layouts: 4.73 us -> 2.9 us
where the time goes in v2:
time: 118 us; the launch traced here: 117 us
  Pallas kernels  114 us (97%)
  local copies, waits for them, and re-layouts  2.9 us (2%)
    pallas_call x1, Pallas kernels, communicate(): pl.pallas_call(functools.partial(comm_kernel, nz, nx), out_shape=(jax.Sha...  92.4 us
    pallas_call x1, Pallas kernels, finish(): pl.pallas_call(functools.partial(factor_kernel, scale), out_shape=(jax.Sh...  21.3 us
    unnamed x4, local copies, waits for them, and re-layouts  2.9 us

profile of v2, /device:TPU:1, one launch (start us, length us, event | category | flops | bytes accessed | tf_op | source)
XLA Modules:
  0.0 117.3 jit_solution(141122526998189400)
XLA Ops:
  0.6 0.0 copy-start
  0.6 2.2 %copy-done = bf16[1024,2048]{1,0:T(8,128)(2,1)S(1)} copy-done((bf16[1024,2048]{1,0:T(8,128)(2,1)S(1)}, bf16[1024,2048]{1,0:T(8,128)(2,1)}, u32[]{:S(2)}) %copy-start) | copy-done | bytes 4194328
  2.8 0.0 copy-start.1
  2.8 0.7 copy-done.1
  3.5 92.4 %shard_map.41 = (f32[256,512]{1,0:T(8,128)S(1)}, f32[3,2,16,8,256]{4,3,2,1,0:T(8,128)S(1)}) custom-call(bf16[1024,2048]{1,0:T(8,128)(2,1)S(1)} %copy-done, bf16[16,512]{1,0:T(8,128)(2,1)S(1)} %copy-done.1), custom_call_target="tpu_custom_call" | custom-call | tf_op jit(solution)/shard_map/pallas_call | solution.py:251
  96.0 21.3 %shard_map.42 = (f32[256,512]{1,0:T(8,128)}, f32[128,512]{1,0:T(8,128)}) custom-call(f32[256,512]{1,0:T(8,128)S(1)} %get-tuple-element.4.s_ref, f32[3,2,128,256]{3,2,1,0:T(8,128)S(1)} %bitcast.1), custom_call_target="tpu_custom_call" | custom-call | tf_op jit(solution)/shard_map/pallas_call | solution.py:380
Async XLA Ops:
  0.6 2.2 %copy-start = (bf16[1024,2048]{1,0:T(8,128)(2,1)S(1)}, bf16[1024,2048]{1,0:T(8,128)(2,1)}, u32[]{:S(2)}) copy-start(bf16[1024,2048]{1,0:T(8,128)(2,1)} %a_hbm.1) | copy-start | bytes 12582916
  2.8 0.7 copy-start.1

commit v3 on v1

v3 whole, which is shorter than its diff:
```python
import functools
import jax
import jax.numpy as jnp
from jax import lax
from jax.experimental import pallas as pl
from jax.experimental.pallas import tpu as pltpu
from jax.sharding import PartitionSpec as P

NY = 4
NC = 2
W = 128
CHUNKS = 4
VMEM_MIB = 40
MESH = pl.DeviceIdType.MESH


HIGHEST = lax.Precision.HIGHEST


def mm(a, b, ca, cb):
    return lax.dot_general(a, b, (((ca,), (cb,)), ((), ())), precision=HIGHEST, preferred_element_type=jnp.float32)


def factor_block(w_ref, q_ref, hooks=None):
    n = W // 8
    sub = lax.broadcasted_iota(jnp.int32, (8, W), 0)
    lane = lax.broadcasted_iota(jnp.int32, (8, W), 1)

    def along(v, i):
        return jnp.broadcast_to(v[:, i : i + 1], (8, W))

    def down(v, i):
        return jnp.broadcast_to(v[i : i + 1, :], (8, W))

    for t in range(n):
        q_ref[8 * t : 8 * t + 8, :] = jnp.where(lane == sub + 8 * t, 1.0, 0.0).astype(jnp.float32)
    for k in range(n):
        if hooks and k in hooks:
            hooks[k]()
        p = w_ref[8 * k : 8 * k + 8, :]
        q = q_ref[8 * k : 8 * k + 8, :]
        cols = [along(p, 8 * k + m) for m in range(8)]
        rinv, below, us, qs = [], [], [], []
        for m in range(8):
            ri = lax.rsqrt(down(cols[m], m))
            l = cols[m] * ri
            pivots = {}
            for i in range(m + 1, 8):
                pivots[i] = down(l, i)
                cols[i] = cols[i] - l * pivots[i]
            lm = jnp.where(sub > m, l, 0.0)
            u = down(p, m) * ri
            v = down(q, m) * ri
            p = jnp.where(sub == m, u, p - lm * u)
            q = jnp.where(sub == m, v, q - lm * v)
            rinv.append(ri)
            below.append(pivots)
            us.append(u)
            qs.append(v)
        w_ref[8 * k : 8 * k + 8, :] = p
        q_ref[8 * k : 8 * k + 8, :] = q
        for t in range(k + 1, n):
            wt = w_ref[8 * t : 8 * t + 8, :]
            qt = q_ref[8 * t : 8 * t + 8, :]
            ct = [along(wt, 8 * k + m) for m in range(8)]
            for m in range(8):
                l = ct[m] * rinv[m]
                for i in range(m + 1, 8):
                    ct[i] = ct[i] - l * below[m][i]
                wt = wt - l * us[m]
                qt = qt - l * qs[m]
            w_ref[8 * t : 8 * t + 8, :] = wt
            q_ref[8 * t : 8 * t + 8, :] = qt


def sketch_kernel(nz, nx, scale, a_hbm, t_ref, basis_ref, out_ref, a_v, tg, part, rsr, s_ref, own, crecv, hb, prs, zr, fin, left, low, upper, diag, w_ref, q_ref, a_sem, zs, ys, ks, rs, cs, ps, gz, ag, ck):
    ny = NY
    r = lax.axis_index("row")
    x = lax.axis_index("col")
    c = lax.rem(r, NC)
    y = lax.rem(r // NC, ny)
    z = r // (NC * ny)
    ns = ny * nx
    s = y * nx + x
    share = s_ref.shape[0]

    def row_of(zz, yy, cc):
        return (zz * ny + yy) * NC + cc

    def z_peer(i):
        return (row_of(lax.rem(z + i, nz), y, c), x)

    nu = 2 * ns
    zb = lax.rem(z, 2)
    zp = z // 2
    nzp = nz // 2
    u = zb * ns + s

    def pair_peer(i):
        v = lax.rem(u + i, nu)
        q = lax.rem(v, ns)
        return v, (row_of(2 * zp + v // ns, q // nx, c), lax.rem(q, nx))

    def far_peer(i):
        return (row_of(2 * lax.rem(zp + i, nzp) + zb, y, c), x)

    sibling = (row_of(z, y, 1 - c), x)

    load_a = pltpu.make_async_copy(a_hbm, a_v, a_sem)
    load_a.start()
    barrier = pltpu.get_barrier_semaphore()

    def greet_z(i, carry):
        pl.semaphore_signal(barrier, inc=1, device_id=z_peer(i), device_id_type=MESH)
        return carry

    def greet_pair(i, carry):
        pl.semaphore_signal(barrier, inc=1, device_id=pair_peer(i)[1], device_id_type=MESH)
        return carry

    lax.fori_loop(1, nz, greet_z, 0)
    lax.fori_loop(1, nu, greet_pair, 0)
    pl.semaphore_signal(barrier, inc=1, device_id=sibling, device_id_type=MESH)
    for j in range(CHUNKS):
        tg[j, z, y, c] = t_ref[:, j * W : (j + 1) * W]
    pl.semaphore_wait(barrier, nz + nu - 1)

    def rcopy(src, dst, sems, k, to):
        return pltpu.make_async_remote_copy(
            src_ref=src, dst_ref=dst, send_sem=sems.at[0, k], recv_sem=sems.at[1, k],
            device_id=to, device_id_type=MESH,
        )

    def wait_bytes(view, sem):
        pltpu.make_async_copy(view, view, sem).wait()

    def z_send(j):
        def body(i, carry):
            rcopy(t_ref.at[:, pl.ds(j * W, W)], tg.at[j, z, y, c], zs, j, z_peer(i)).start()
            return carry
        lax.fori_loop(1, nz, body, 0)

    def z_view(j):
        return tg.at[j, pl.ds(0, nz - 1), y, c]

    def y_send(j):
        def body(i, carry):
            rcopy(tg.at[j, :, y, c], tg.at[j, :, y, c], ys, j, (row_of(z, lax.rem(y + i, ny), c), x)).start()
            return carry
        lax.fori_loop(1, ny, body, 0)

    def y_view(j):
        return tg.at[j, :, pl.ds(0, ny - 1), c]

    def k_copy(j):
        return rcopy(tg.at[j, :, :, c], tg.at[j, :, :, c], ks, j, sibling)

    def project(j):
        t_all = tg[j].reshape(-1, W)

        def block(d):
            q = lax.rem(x + d, nx)
            rows = pl.ds(pl.multiple_of(q * share, share), share)
            return q, jnp.dot(a_v[rows, :], t_all, preferred_element_type=jnp.float32)

        def body(i, carry):
            d = nx - 1 - i
            q, value = block(d)
            part[j, d] = value
            rcopy(part.at[j, d], rsr.at[j, d - 1], rs, j, (r, q)).start()
            return carry
        lax.fori_loop(0, nx - 1, body, 0)
        part[j, 0] = block(0)[1]

    def rs_view(j):
        return rsr.at[j]

    def finish_chunk(j):
        wait_bytes(rs_view(j), rs.at[1, j])
        total = part[j, 0]
        for d in range(nx - 1):
            total = total + rsr[j, d]
        s_ref[:, j * W : (j + 1) * W] = total

    def gram_block(i, j):
        return lax.dot_general(
            s_ref[:, i * W : (i + 1) * W], s_ref[:, j * W : (j + 1) * W], (((0,), (0,)), ((), ())),
            precision=lax.Precision.HIGHEST, preferred_element_type=jnp.float32,
        )

    places = {
        0: [[(0, 0), (0, 1)], [(1, 0), (1, 1)]],
        1: [[(2, 0), (2, 1)], [(2, 2), None]],
        2: [[(3, 0), (3, 1)], [(3, 2), (3, 3)]],
    }

    def gram(g):
        for half in range(2):
            for k in range(2):
                place = places[g][half][k]
                own[g, half, k] = jnp.zeros((W, W), jnp.float32) if place is None else gram_block(*place)
        rcopy(own.at[g, 1 - c], crecv.at[g], cs, g, sibling).start()

    def pair_send(g):
        wait_bytes(crecv.at[g], cs.at[1, g])
        hb[g] = (own[g, c] + crecv[g]).reshape(hb.shape[1:])

        def body(i, carry):
            v, to = pair_peer(i)
            rcopy(hb.at[g, v], prs.at[g, u], ps, g, to).start()
            return carry
        lax.fori_loop(1, nu, body, 0)
        prs[g, u] = hb[g, u]

    def pair_view(g):
        return prs.at[g, pl.ds(0, nu - 1)]

    def far_send(g):
        wait_bytes(pair_view(g), ps.at[1, g])
        zr[g, zp] = jnp.sum(prs[g], axis=0)

        def body(i, carry):
            rcopy(zr.at[g, zp], zr.at[g, zp], gz, g, far_peer(i)).start()
            return carry
        lax.fori_loop(1, nzp, body, 0)

    def far_view(g):
        return zr.at[g, pl.ds(0, nzp - 1)]

    def spread(g):
        wait_bytes(far_view(g), gz.at[1, g])
        fin[g, c, u] = jnp.sum(zr[g], axis=0)

        def body(i, carry):
            rcopy(fin.at[g, c, u], fin.at[g, c, u], ag, g, pair_peer(i)[1]).start()
            return carry
        lax.fori_loop(1, nu, body, 0)

    def spread_view(g):
        return fin.at[g, c, pl.ds(0, nu - 1)]

    def spread_core(g):
        wait_bytes(spread_view(g), ag.at[1, g])
        rcopy(fin.at[g, c], fin.at[g, c], ck, g, sibling).start()

    def spread_end(g):
        wait_bytes(fin.at[g, c], ck.at[1, g])

    row_at = lax.broadcasted_iota(jnp.int32, (W, W), 0)
    col_at = lax.broadcasted_iota(jnp.int32, (W, W), 1)
    done = []
    arrived = []

    def catch_up(j, b):
        l = mm(left[j, b], diag[b], 1, 1)
        low[j, b] = l
        for i in range(b + 1, j + 1):
            left[j, i] = left[j, i] - mm(l, low[i, b], 1, 1)

    def settle(j, b):
        l = low[j, b]
        upper[b, :, j * W : (j + 1) * W] = l.T
        block = (slice(None), slice(j * W, (j + 1) * W))
        basis_ref[block] = basis_ref[block] - mm(basis_ref[:, b * W : (b + 1) * W], l, 1, 1)

    def arrive(j):
        if j < 2:
            g, half = 0, j
        else:
            g = j - 1
        for i in range(j + 1):
            f, k = (half, i) if j < 2 else (i // 2, i % 2)
            left[j, i] = fin[g, f, k * ns : (k + 1) * ns].reshape(W, W) * scale
        basis_ref[:, j * W : (j + 1) * W] = s_ref[:, j * W : (j + 1) * W]
        arrived.append(j)
        for b in done:
            catch_up(j, b)
        for b in done:
            settle(j, b)

    def factor(b, hooks=None):
        w_ref[...] = left[b, b]
        factor_block(w_ref, q_ref, hooks)
        q = q_ref[...]
        diag[b] = q
        upper[b, :, b * W : (b + 1) * W] = jnp.where(col_at >= row_at, w_ref[...], 0.0)
        later = [j for j in arrived if j > b]
        for j in later:
            catch_up(j, b)
        block = (slice(None), slice(b * W, (b + 1) * W))
        basis_ref[block] = mm(basis_ref[block], q, 1, 1)
        for j in later:
            settle(j, b)
        done.append(b)

    for j in range(CHUNKS):
        z_send(j)

    def do_z(j):
        wait_bytes(z_view(j), zs.at[1, j])
        y_send(j)

    def do_y(j):
        wait_bytes(y_view(j), ys.at[1, j])
        k_copy(j).start()

    def do_k(j):
        wait_bytes(tg.at[j, :, :, c], ks.at[1, j])
        project(j)

    do_z(0)
    do_z(1)
    do_z(2)
    do_y(0)
    do_z(3)
    load_a.wait()
    do_k(0)
    do_y(1)
    do_k(1)
    do_y(2)
    do_k(2)
    do_y(3)
    do_k(3)
    finish_chunk(0)
    finish_chunk(1)
    gram(0)
    pair_send(0)
    finish_chunk(2)
    gram(1)
    pair_send(1)
    far_send(0)
    finish_chunk(3)
    gram(2)
    pair_send(2)
    far_send(1)
    spread(0)
    far_send(2)
    upper[...] = jnp.zeros_like(upper)
    spread(1)
    spread_core(0)
    spread_end(0)
    arrive(0)
    arrive(1)
    factor(0)
    spread(2)
    spread_core(1)
    factor(1)
    spread_end(1)
    arrive(2)

    def last_group():
        spread_core(2)

    factor(2, {8: last_group})
    spread_end(2)
    arrive(3)
    factor(3)
    out_ref[...] = upper[x]

    for j in range(CHUNKS):
        wait_bytes(z_view(j), zs.at[0, j])
        wait_bytes(y_view(j), ys.at[0, j])
        wait_bytes(tg.at[j, :, :, c], ks.at[0, j])
        wait_bytes(rs_view(j), rs.at[0, j])
    for g in range(3):
        wait_bytes(crecv.at[g], cs.at[0, g])
        wait_bytes(pair_view(g), ps.at[0, g])
        wait_bytes(far_view(g), gz.at[0, g])
        wait_bytes(spread_view(g), ag.at[0, g])
        wait_bytes(fin.at[g, c], ck.at[0, g])


def solution(mesh):
    nx = mesh.shape["col"]
    nz = mesh.shape["row"] // (NY * NC)
    ns = NY * nx
    pr = W // ns
    f32 = jnp.float32
    dma = pltpu.SemaphoreType.DMA

    def on_device(travel_times, test_matrix):
        rows, cols = travel_times.shape
        depth, width = test_matrix.shape
        share = rows // nx
        scale = 1.0 / (rows * mesh.shape["row"])
        return pl.pallas_call(
            functools.partial(sketch_kernel, nz, nx, scale),
            out_shape=(
                jax.ShapeDtypeStruct((share, width), f32),
                jax.ShapeDtypeStruct((width // nx, width), f32),
            ),
            in_specs=[pl.BlockSpec(memory_space=pl.ANY), pl.BlockSpec(memory_space=pltpu.VMEM)],
            out_specs=[pl.BlockSpec(memory_space=pltpu.VMEM)] * 2,
            scratch_shapes=[
                pltpu.VMEM((rows, cols), jnp.bfloat16),
                pltpu.VMEM((CHUNKS, nz, NY, NC, depth, W), jnp.bfloat16),
                pltpu.VMEM((CHUNKS, nx, share, W), f32),
                pltpu.VMEM((CHUNKS, nx - 1, share, W), f32),
                pltpu.VMEM((share, width), f32),
                pltpu.VMEM((3, 2, 2, W, W), f32),
                pltpu.VMEM((3, 2, W, W), f32),
                pltpu.VMEM((3, 2 * ns, pr, W), f32),
                pltpu.VMEM((3, 2 * ns, pr, W), f32),
                pltpu.VMEM((3, nz // 2, pr, W), f32),
                pltpu.VMEM((3, 2, 2 * ns, pr, W), f32),
                pltpu.VMEM((CHUNKS, CHUNKS, W, W), f32),
                pltpu.VMEM((CHUNKS, CHUNKS, W, W), f32),
                pltpu.VMEM((CHUNKS, W, width), f32),
                pltpu.VMEM((CHUNKS, W, W), f32),
                pltpu.VMEM((W, W), f32),
                pltpu.VMEM((W, W), f32),
                dma,
            ]
            + [dma((2, CHUNKS))] * 4
            + [dma((2, 3))] * 5,
            compiler_params=pltpu.CompilerParams(
                collective_id=0, has_side_effects=True, vmem_limit_bytes=VMEM_MIB << 20
            ),
        )(travel_times, test_matrix)

    return jax.shard_map(
        on_device, mesh=mesh, in_specs=(P("row", "col"), P(("col", "row"), None)),
        out_specs=(P(("row", "col"), None), P("col", None)), check_vma=False,
    )
```

time: 235 us -> 105 us (0.45)
  other arithmetic: 120 us -> 0 us
  local copies, waits for them, and re-layouts: 14.3 us -> 4.4 us
  Pallas kernels: 92.4 us -> 99.3 us
  matrix products: 4.91 us -> 0 us
  between operations: 3.44 us -> 0.65 us
    another operation x17 -> x0, other arithmetic: 119 us -> none  [the longest x14 78.5 us: on_device(): lower = lax.linalg.cholesky(gram_mean, symmetrize_input=False)]
    another operation x17 -> x0, local copies, waits for them, and re-layouts: 8.53 us -> none
    pallas_call x1, Pallas kernels: 92.4 us -> 99.3 us  [on_device(): pl.pallas_call(functools.partial(sketch_kernel, nz, nx, scale), out_shape...]
    another operation x13 -> x0, matrix products: 4.91 us -> none  [the longest x7 3.03 us: on_device(): basis = jax.scipy.linalg.solve_triangular(lower, sketch.T, lower=True).T]
where the time goes in v3:
time: 105 us; the launch traced here: 104 us
  Pallas kernels  99.3 us (95%)
  local copies, waits for them, and re-layouts  4.4 us (4%)
    pallas_call x1, Pallas kernels, on_device(): pl.pallas_call(functools.partial(sketch_kernel, nz, nx, scale), out_shape...  99.3 us
    unnamed x6, local copies, waits for them, and re-layouts  4.4 us

profile of v3, /device:TPU:1, one launch (start us, length us, event | category | flops | bytes accessed | tf_op | source)
XLA Modules:
  0.0 104.3 jit_solution(13261956657830489315)
XLA Ops:
  0.6 0.0 copy-start
  0.6 2.2 %copy-done = bf16[1024,2048]{1,0:T(8,128)(2,1)S(1)} copy-done((bf16[1024,2048]{1,0:T(8,128)(2,1)S(1)}, bf16[1024,2048]{1,0:T(8,128)(2,1)}, u32[]{:S(2)}) %copy-start) | copy-done | bytes 4194328
  2.8 0.0 copy-start.1
  2.8 0.7 copy-done.1
  3.5 99.3 %shard_map.41 = (f32[256,512]{1,0:T(8,128)S(1)}, f32[128,512]{1,0:T(8,128)S(1)}) custom-call(bf16[1024,2048]{1,0:T(8,128)(2,1)S(1)} %copy-done, bf16[16,512]{1,0:T(8,128)(2,1)S(1)} %copy-done.1), custom_call_target="tpu_custom_call" | custom-call | tf_op jit(solution)/shard_map/pallas_call | solution.py:386
  102.8 0.8 copy.6
  103.6 0.7 copy.7
Async XLA Ops:
  0.6 2.2 %copy-start = (bf16[1024,2048]{1,0:T(8,128)(2,1)S(1)}, bf16[1024,2048]{1,0:T(8,128)(2,1)}, u32[]{:S(2)}) copy-start(bf16[1024,2048]{1,0:T(8,128)(2,1)} %a_hbm.1) | copy-start | bytes 12582916
  2.8 0.7 copy-start.1

commit v4 on v3

--- a/solution.py
+++ b/solution.py
@@ -10,7 +10,7 @@
 NC = 2
 W = 128
 CHUNKS = 4
-VMEM_MIB = 40
+VMEM_MIB = 58
 MESH = pl.DeviceIdType.MESH
 
 
@@ -34,12 +34,21 @@
 
     for t in range(n):
         q_ref[8 * t : 8 * t + 8, :] = jnp.where(lane == sub + 8 * t, 1.0, 0.0).astype(jnp.float32)
+    first = w_ref[0:8, :]
+    cols = [along(first, m) for m in range(8)]
     for k in range(n):
         if hooks and k in hooks:
             hooks[k]()
-        p = w_ref[8 * k : 8 * k + 8, :]
-        q = q_ref[8 * k : 8 * k + 8, :]
-        cols = [along(p, 8 * k + m) for m in range(8)]
+        here = slice(8 * k, 8 * k + 8)
+        after = slice(8 * k + 8, 8 * k + 16)
+        p = w_ref[here, :]
+        q = q_ref[here, :]
+        more = k + 1 < n
+        if more:
+            wn = w_ref[after, :]
+            qn = q_ref[after, :]
+            cn = [along(wn, 8 * k + m) for m in range(8)]
+            dn = [along(wn, 8 * k + 8 + m) for m in range(8)]
         rinv, below, us, qs = [], [], [], []
         for m in range(8):
             ri = lax.rsqrt(down(cols[m], m))
@@ -57,9 +66,21 @@
             below.append(pivots)
             us.append(u)
             qs.append(v)
-        w_ref[8 * k : 8 * k + 8, :] = p
-        q_ref[8 * k : 8 * k + 8, :] = q
-        for t in range(k + 1, n):
+            if more:
+                ln = cn[m] * ri
+                for i in range(m + 1, 8):
+                    cn[i] = cn[i] - ln * pivots[i]
+                for i in range(8):
+                    dn[i] = dn[i] - ln * down(ln, i)
+                wn = wn - ln * u
+                qn = qn - ln * v
+        w_ref[here, :] = p
+        q_ref[here, :] = q
+        if more:
+            w_ref[after, :] = wn
+            q_ref[after, :] = qn
+            cols = dn
+        for t in range(k + 2, n):
             wt = w_ref[8 * t : 8 * t + 8, :]
             qt = q_ref[8 * t : 8 * t + 8, :]
             ct = [along(wt, 8 * k + m) for m in range(8)]
@@ -182,28 +203,25 @@
             total = total + rsr[j, d]
         s_ref[:, j * W : (j + 1) * W] = total
 
-    def gram_block(i, j):
-        return lax.dot_general(
-            s_ref[:, i * W : (i + 1) * W], s_ref[:, j * W : (j + 1) * W], (((0,), (0,)), ((), ())),
-            precision=lax.Precision.HIGHEST, preferred_element_type=jnp.float32,
+    def gram(g):
+        n = (g + 1) * W
+        value = lax.dot_general(
+            s_ref[:, g * W : n], s_ref[:, 0:n], (((0,), (0,)), ((), ())),
+            precision=HIGHEST, preferred_element_type=jnp.float32,
         )
-
-    places = {
-        0: [[(0, 0), (0, 1)], [(1, 0), (1, 1)]],
-        1: [[(2, 0), (2, 1)], [(2, 2), None]],
-        2: [[(3, 0), (3, 1)], [(3, 2), (3, 3)]],
-    }
-
-    def gram(g):
-        for half in range(2):
-            for k in range(2):
-                place = places[g][half][k]
-                own[g, half, k] = jnp.zeros((W, W), jnp.float32) if place is None else gram_block(*place)
-        rcopy(own.at[g, 1 - c], crecv.at[g], cs, g, sibling).start()
+        for i in range(g + 1):
+            own[g, i // 2, i % 2] = value[:, i * W : (i + 1) * W]
+        if g % 2 == 0:
+            own[g, g // 2, 1] = jnp.zeros((W, W), jnp.float32)
+        if g >= 2:
+            rcopy(own.at[g, 1 - c], crecv.at[g - 2], cs, g - 2, sibling).start()
 
     def pair_send(g):
-        wait_bytes(crecv.at[g], cs.at[1, g])
-        hb[g] = (own[g, c] + crecv[g]).reshape(hb.shape[1:])
+        if g >= 2:
+            wait_bytes(crecv.at[g - 2], cs.at[1, g - 2])
+            hb[g] = (own[g, c] + crecv[g - 2]).reshape(hb.shape[1:])
+        else:
+            hb[g] = own[g, 0].reshape(hb.shape[1:])
 
         def body(i, carry):
             v, to = pair_peer(i)
@@ -264,13 +282,10 @@
         basis_ref[block] = basis_ref[block] - mm(basis_ref[:, b * W : (b + 1) * W], l, 1, 1)
 
     def arrive(j):
-        if j < 2:
-            g, half = 0, j
-        else:
-            g = j - 1
         for i in range(j + 1):
-            f, k = (half, i) if j < 2 else (i // 2, i % 2)
-            left[j, i] = fin[g, f, k * ns : (k + 1) * ns].reshape(W, W) * scale
+            f, k = i // 2, slice((i % 2) * ns, (i % 2 + 1) * ns)
+            tiles = fin[j, f, k] if j >= 2 else fin[j, 0, k] + fin[j, 1, k]
+            left[j, i] = tiles.reshape(W, W) * scale
         basis_ref[:, j * W : (j + 1) * W] = s_ref[:, j * W : (j + 1) * W]
         arrived.append(j)
         for b in done:
@@ -322,37 +337,49 @@
     do_y(3)
     do_k(3)
     finish_chunk(0)
-    finish_chunk(1)
     gram(0)
     pair_send(0)
-    finish_chunk(2)
+    upper[...] = jnp.zeros_like(upper)
+    finish_chunk(1)
     gram(1)
     pair_send(1)
     far_send(0)
+    finish_chunk(2)
+    gram(2)
+    far_send(1)
+    pair_send(2)
+    spread(0)
     finish_chunk(3)
-    gram(2)
-    pair_send(2)
-    far_send(1)
-    spread(0)
+    gram(3)
+    pair_send(3)
     far_send(2)
-    upper[...] = jnp.zeros_like(upper)
     spread(1)
     spread_core(0)
     spread_end(0)
     arrive(0)
+
+    def early():
+        far_send(3)
+
+    def middle():
+        spread_core(1)
+        spread(2)
+
+    factor(0, {2: early, 14: middle})
+    spread_end(1)
     arrive(1)
-    factor(0)
-    spread(2)
-    spread_core(1)
-    factor(1)
-    spread_end(1)
+
+    def third():
+        spread_core(2)
+
+    def fourth():
+        spread(3)
+
+    factor(1, {8: fourth, 13: third})
+    spread_end(2)
     arrive(2)
-
-    def last_group():
-        spread_core(2)
-
-    factor(2, {8: last_group})
-    spread_end(2)
+    factor(2, {14: lambda: spread_core(3)})
+    spread_end(3)
     arrive(3)
     factor(3)
     out_ref[...] = upper[x]
@@ -362,8 +389,9 @@
         wait_bytes(y_view(j), ys.at[0, j])
         wait_bytes(tg.at[j, :, :, c], ks.at[0, j])
         wait_bytes(rs_view(j), rs.at[0, j])
-    for g in range(3):
+    for g in range(2):
         wait_bytes(crecv.at[g], cs.at[0, g])
+    for g in range(CHUNKS):
         wait_bytes(pair_view(g), ps.at[0, g])
         wait_bytes(far_view(g), gz.at[0, g])
         wait_bytes(spread_view(g), ag.at[0, g])
@@ -397,12 +425,12 @@
                 pltpu.VMEM((CHUNKS, nx, share, W), f32),
                 pltpu.VMEM((CHUNKS, nx - 1, share, W), f32),
                 pltpu.VMEM((share, width), f32),
-                pltpu.VMEM((3, 2, 2, W, W), f32),
-                pltpu.VMEM((3, 2, W, W), f32),
-                pltpu.VMEM((3, 2 * ns, pr, W), f32),
-                pltpu.VMEM((3, 2 * ns, pr, W), f32),
-                pltpu.VMEM((3, nz // 2, pr, W), f32),
-                pltpu.VMEM((3, 2, 2 * ns, pr, W), f32),
+                pltpu.VMEM((CHUNKS, 2, 2, W, W), f32),
+                pltpu.VMEM((2, 2, W, W), f32),
+                pltpu.VMEM((CHUNKS, 2 * ns, pr, W), f32),
+                pltpu.VMEM((CHUNKS, 2 * ns, pr, W), f32),
+                pltpu.VMEM((CHUNKS, nz // 2, pr, W), f32),
+                pltpu.VMEM((CHUNKS, 2, 2 * ns, pr, W), f32),
                 pltpu.VMEM((CHUNKS, CHUNKS, W, W), f32),
                 pltpu.VMEM((CHUNKS, CHUNKS, W, W), f32),
                 pltpu.VMEM((CHUNKS, W, width), f32),
@@ -412,7 +440,8 @@
                 dma,
             ]
             + [dma((2, CHUNKS))] * 4
-            + [dma((2, 3))] * 5,
+            + [dma((2, 2))]
+            + [dma((2, CHUNKS))] * 4,
             compiler_params=pltpu.CompilerParams(
                 collective_id=0, has_side_effects=True, vmem_limit_bytes=VMEM_MIB << 20
             ),

time: 105 us -> 104 us (level)
    unnamed x6 -> x2, local copies, waits for them, and re-layouts: 4.4 us -> 3.54 us
where the time goes in v4:
time: 104 us
  Pallas kernels  100 us (96%)
  local copies, waits for them, and re-layouts  3.54 us (3%)
    pallas_call x1, Pallas kernels, on_device(): pl.pallas_call(functools.partial(sketch_kernel, nz, nx, scale), out_shape...  100 us
    unnamed x2, local copies, waits for them, and re-layouts  3.54 us

profile of v4, /device:TPU:1, one launch (start us, length us, event | category | flops | bytes accessed | tf_op | source)
XLA Modules:
  0.0 104.1 jit_solution(8590083377329391746)
XLA Ops:
  0.6 100.0 %shard_map.41 = (f32[256,512]{1,0:T(8,128)}, f32[128,512]{1,0:T(8,128)}) custom-call(bf16[1024,2048]{1,0:T(8,128)(2,1)} %a_hbm.1, bf16[16,512]{1,0:T(8,128)(2,1)} %t_ref.1), custom_call_target="tpu_custom_call" | custom-call | tf_op jit(solution)/shard_map/pallas_call | solution.py:414
  100.6 1.9 %copy.6 = f32[256,512]{1,0:T(8,128)} copy(f32[256,512]{1,0:T(8,128)} %get-tuple-element.4) | data formatting | bytes 1048576
  102.5 1.7 %copy.7 = f32[128,512]{1,0:T(8,128)} copy(f32[128,512]{1,0:T(8,128)} %get-tuple-element.5) | data formatting | bytes 524288

commit v5 on v3

--- a/solution.py
+++ b/solution.py
@@ -10,7 +10,7 @@
 NC = 2
 W = 128
 CHUNKS = 4
-VMEM_MIB = 40
+VMEM_MIB = 58
 MESH = pl.DeviceIdType.MESH
 
 
@@ -34,12 +34,21 @@
 
     for t in range(n):
         q_ref[8 * t : 8 * t + 8, :] = jnp.where(lane == sub + 8 * t, 1.0, 0.0).astype(jnp.float32)
+    first = w_ref[0:8, :]
+    cols = [along(first, m) for m in range(8)]
     for k in range(n):
         if hooks and k in hooks:
             hooks[k]()
-        p = w_ref[8 * k : 8 * k + 8, :]
-        q = q_ref[8 * k : 8 * k + 8, :]
-        cols = [along(p, 8 * k + m) for m in range(8)]
+        here = slice(8 * k, 8 * k + 8)
+        after = slice(8 * k + 8, 8 * k + 16)
+        p = w_ref[here, :]
+        q = q_ref[here, :]
+        more = k + 1 < n
+        if more:
+            wn = w_ref[after, :]
+            qn = q_ref[after, :]
+            cn = [along(wn, 8 * k + m) for m in range(8)]
+            dn = [along(wn, 8 * k + 8 + m) for m in range(8)]
         rinv, below, us, qs = [], [], [], []
         for m in range(8):
             ri = lax.rsqrt(down(cols[m], m))
@@ -57,9 +66,21 @@
             below.append(pivots)
             us.append(u)
             qs.append(v)
-        w_ref[8 * k : 8 * k + 8, :] = p
-        q_ref[8 * k : 8 * k + 8, :] = q
-        for t in range(k + 1, n):
+            if more:
+                ln = cn[m] * ri
+                for i in range(m + 1, 8):
+                    cn[i] = cn[i] - ln * pivots[i]
+                for i in range(8):
+                    dn[i] = dn[i] - ln * down(ln, i)
+                wn = wn - ln * u
+                qn = qn - ln * v
+        w_ref[here, :] = p
+        q_ref[here, :] = q
+        if more:
+            w_ref[after, :] = wn
+            q_ref[after, :] = qn
+            cols = dn
+        for t in range(k + 2, n):
             wt = w_ref[8 * t : 8 * t + 8, :]
             qt = q_ref[8 * t : 8 * t + 8, :]
             ct = [along(wt, 8 * k + m) for m in range(8)]
@@ -73,7 +94,7 @@
             q_ref[8 * t : 8 * t + 8, :] = qt
 
 
-def sketch_kernel(nz, nx, scale, a_hbm, t_ref, basis_ref, out_ref, a_v, tg, part, rsr, s_ref, own, crecv, hb, prs, zr, fin, left, low, upper, diag, w_ref, q_ref, a_sem, zs, ys, ks, rs, cs, ps, gz, ag, ck):
+def sketch_kernel(nz, nx, scale, a_hbm, t_ref, basis_ref, out_ref, a_v, tg, part, rsr, s_ref, own, crecv, hb, prs, zr, fin, left, low, upper, diag, w_ref, q_ref, a_sem, zs, ys, ks, rq, rs, cs, ps, gz, ag, ck):
     ny = NY
     r = lax.axis_index("row")
     x = lax.axis_index("col")
@@ -155,50 +176,69 @@
     def k_copy(j):
         return rcopy(tg.at[j, :, :, c], tg.at[j, :, :, c], ks, j, sibling)
 
+    half_rows = share // 2
+    top = pl.ds(0, half_rows)
+    bottom = pl.ds(half_rows, half_rows)
+    right = (r, lax.rem(x + 1, nx))
+    left_dev = (r, lax.rem(x + nx - 1, nx))
+
     def project(j):
         t_all = tg[j].reshape(-1, W)
 
-        def block(d):
+        def body(i, carry):
+            d = lax.rem(i + 2, nx)
             q = lax.rem(x + d, nx)
             rows = pl.ds(pl.multiple_of(q * share, share), share)
-            return q, jnp.dot(a_v[rows, :], t_all, preferred_element_type=jnp.float32)
-
-        def body(i, carry):
-            d = nx - 1 - i
-            q, value = block(d)
-            part[j, d] = value
-            rcopy(part.at[j, d], rsr.at[j, d - 1], rs, j, (r, q)).start()
-            return carry
-        lax.fori_loop(0, nx - 1, body, 0)
-        part[j, 0] = block(0)[1]
+            part[j, d] = jnp.dot(a_v[rows, :], t_all, preferred_element_type=jnp.float32)
+
+            @pl.when(i == 0)
+            def _():
+                rcopy(part.at[j, 2, top], rsr.at[j, 0], rq, j, right).start()
+                rcopy(part.at[j, 2, bottom], rsr.at[j, 1], rq, j, left_dev).start()
+
+            @pl.when(i == 1)
+            def _():
+                rcopy(part.at[j, 3, top], rsr.at[j, 2], rs, j, left_dev).start()
+
+            @pl.when(i == 3)
+            def _():
+                rcopy(part.at[j, 1, bottom], rsr.at[j, 3], rs, j, right).start()
+            return carry
+        lax.fori_loop(0, nx, body, 0)
+
+    def relay(j):
+        wait_bytes(relay_view(j), rq.at[1, j])
+        part[j, 1, top] = part[j, 1, top] + rsr[j, 0]
+        rcopy(part.at[j, 1, top], rsr.at[j, 4], rs, j, right).start()
+        part[j, 3, bottom] = part[j, 3, bottom] + rsr[j, 1]
+        rcopy(part.at[j, 3, bottom], rsr.at[j, 5], rs, j, left_dev).start()
+
+    def relay_view(j):
+        return rsr.at[j, pl.ds(0, 2)]
 
     def rs_view(j):
-        return rsr.at[j]
+        return rsr.at[j, pl.ds(2, 4)]
 
     def finish_chunk(j):
         wait_bytes(rs_view(j), rs.at[1, j])
-        total = part[j, 0]
-        for d in range(nx - 1):
-            total = total + rsr[j, d]
-        s_ref[:, j * W : (j + 1) * W] = total
-
-    def gram_block(i, j):
-        return lax.dot_general(
-            s_ref[:, i * W : (i + 1) * W], s_ref[:, j * W : (j + 1) * W], (((0,), (0,)), ((), ())),
-            precision=lax.Precision.HIGHEST, preferred_element_type=jnp.float32,
+        cols = slice(j * W, (j + 1) * W)
+        s_ref[:half_rows, cols] = (part[j, 0, top] + rsr[j, 2]) + rsr[j, 4]
+        s_ref[half_rows:, cols] = (part[j, 0, bottom] + rsr[j, 3]) + rsr[j, 5]
+
+    def gram(g):
+        start = 0 if g == 0 else (g + 1) * W
+        n = (g + 2) * W
+        value = lax.dot_general(
+            s_ref[:, start:n], s_ref[:, 0:n], (((0,), (0,)), ((), ())),
+            precision=HIGHEST, preferred_element_type=jnp.float32,
         )
-
-    places = {
-        0: [[(0, 0), (0, 1)], [(1, 0), (1, 1)]],
-        1: [[(2, 0), (2, 1)], [(2, 2), None]],
-        2: [[(3, 0), (3, 1)], [(3, 2), (3, 3)]],
-    }
-
-    def gram(g):
         for half in range(2):
             for k in range(2):
-                place = places[g][half][k]
-                own[g, half, k] = jnp.zeros((W, W), jnp.float32) if place is None else gram_block(*place)
+                i, j = (half, k) if g == 0 else (0, 2 * half + k)
+                if j <= (i if g == 0 else g + 1):
+                    own[g, half, k] = value[i * W : (i + 1) * W, j * W : (j + 1) * W]
+                else:
+                    own[g, half, k] = jnp.zeros((W, W), jnp.float32)
         rcopy(own.at[g, 1 - c], crecv.at[g], cs, g, sibling).start()
 
     def pair_send(g):
@@ -264,12 +304,9 @@
         basis_ref[block] = basis_ref[block] - mm(basis_ref[:, b * W : (b + 1) * W], l, 1, 1)
 
     def arrive(j):
-        if j < 2:
-            g, half = 0, j
-        else:
-            g = j - 1
+        g = max(j - 1, 0)
         for i in range(j + 1):
-            f, k = (half, i) if j < 2 else (i // 2, i % 2)
+            f, k = (j, i) if j < 2 else (i // 2, i % 2)
             left[j, i] = fin[g, f, k * ns : (k + 1) * ns].reshape(W, W) * scale
         basis_ref[:, j * W : (j + 1) * W] = s_ref[:, j * W : (j + 1) * W]
         arrived.append(j)
@@ -318,40 +355,41 @@
     do_y(1)
     do_k(1)
     do_y(2)
+    relay(0)
     do_k(2)
     do_y(3)
+    relay(1)
     do_k(3)
+    relay(2)
     finish_chunk(0)
+    upper[...] = jnp.zeros_like(upper)
+    relay(3)
     finish_chunk(1)
     gram(0)
     pair_send(0)
     finish_chunk(2)
     gram(1)
     pair_send(1)
-    far_send(0)
     finish_chunk(3)
     gram(2)
+    far_send(0)
     pair_send(2)
     far_send(1)
+    far_send(2)
     spread(0)
-    far_send(2)
-    upper[...] = jnp.zeros_like(upper)
     spread(1)
     spread_core(0)
     spread_end(0)
+    spread(2)
     arrive(0)
     arrive(1)
     factor(0)
-    spread(2)
     spread_core(1)
     factor(1)
     spread_end(1)
+    spread_core(2)
     arrive(2)
-
-    def last_group():
-        spread_core(2)
-
-    factor(2, {8: last_group})
+    factor(2)
     spread_end(2)
     arrive(3)
     factor(3)
@@ -361,6 +399,7 @@
         wait_bytes(z_view(j), zs.at[0, j])
         wait_bytes(y_view(j), ys.at[0, j])
         wait_bytes(tg.at[j, :, :, c], ks.at[0, j])
+        wait_bytes(relay_view(j), rq.at[0, j])
         wait_bytes(rs_view(j), rs.at[0, j])
     for g in range(3):
         wait_bytes(crecv.at[g], cs.at[0, g])
@@ -395,7 +434,7 @@
                 pltpu.VMEM((rows, cols), jnp.bfloat16),
                 pltpu.VMEM((CHUNKS, nz, NY, NC, depth, W), jnp.bfloat16),
                 pltpu.VMEM((CHUNKS, nx, share, W), f32),
-                pltpu.VMEM((CHUNKS, nx - 1, share, W), f32),
+                pltpu.VMEM((CHUNKS, 6, share // 2, W), f32),
                 pltpu.VMEM((share, width), f32),
                 pltpu.VMEM((3, 2, 2, W, W), f32),
                 pltpu.VMEM((3, 2, W, W), f32),
@@ -411,7 +450,7 @@
                 pltpu.VMEM((W, W), f32),
                 dma,
             ]
-            + [dma((2, CHUNKS))] * 4
+            + [dma((2, CHUNKS))] * 5
             + [dma((2, 3))] * 5,
             compiler_params=pltpu.CompilerParams(
                 collective_id=0, has_side_effects=True, vmem_limit_bytes=VMEM_MIB << 20

time: 105 us -> 96.8 us (0.922)
  Pallas kernels: 99.3 us -> 92.4 us
    pallas_call x1, Pallas kernels: 99.3 us -> 92.4 us  [on_device(): pl.pallas_call(functools.partial(sketch_kernel, nz, nx, scale), out_shape...]
    unnamed x6 -> x2, local copies, waits for them, and re-layouts: 4.4 us -> 3.54 us
where the time goes in v5:
time: 96.8 us; the launch traced here: 96.5 us
  Pallas kernels  92.4 us (95%)
  local copies, waits for them, and re-layouts  3.54 us (4%)
    pallas_call x1, Pallas kernels, on_device(): pl.pallas_call(functools.partial(sketch_kernel, nz, nx, scale), out_shape...  92.4 us
    unnamed x2, local copies, waits for them, and re-layouts  3.54 us

profile of v5, /device:TPU:1, one launch (start us, length us, event | category | flops | bytes accessed | tf_op | source)
XLA Modules:
  0.0 96.5 jit_solution(11964795001423616841)
XLA Ops:
  0.6 92.4 %shard_map.41 = (f32[256,512]{1,0:T(8,128)}, f32[128,512]{1,0:T(8,128)}) custom-call(bf16[1024,2048]{1,0:T(8,128)(2,1)} %a_hbm.1, bf16[16,512]{1,0:T(8,128)(2,1)} %t_ref.1), custom_call_target="tpu_custom_call" | custom-call | tf_op jit(solution)/shard_map/pallas_call | solution.py:425
  93.0 1.9 %copy.6 = f32[256,512]{1,0:T(8,128)} copy(f32[256,512]{1,0:T(8,128)} %get-tuple-element.4) | data formatting | bytes 1048576
  94.9 1.7 %copy.7 = f32[128,512]{1,0:T(8,128)} copy(f32[128,512]{1,0:T(8,128)} %get-tuple-element.5) | data formatting | bytes 524288

commit v6 on v5

--- a/solution.py
+++ b/solution.py
@@ -10,7 +10,7 @@
 NC = 2
 W = 128
 CHUNKS = 4
-VMEM_MIB = 58
+VMEM_MIB = 52
 MESH = pl.DeviceIdType.MESH
 
 
@@ -288,8 +288,6 @@
 
     row_at = lax.broadcasted_iota(jnp.int32, (W, W), 0)
     col_at = lax.broadcasted_iota(jnp.int32, (W, W), 1)
-    done = []
-    arrived = []
 
     def catch_up(j, b):
         l = mm(left[j, b], diag[b], 1, 1)
@@ -297,38 +295,27 @@
         for i in range(b + 1, j + 1):
             left[j, i] = left[j, i] - mm(l, low[i, b], 1, 1)
 
-    def settle(j, b):
-        l = low[j, b]
-        upper[b, :, j * W : (j + 1) * W] = l.T
-        block = (slice(None), slice(j * W, (j + 1) * W))
-        basis_ref[block] = basis_ref[block] - mm(basis_ref[:, b * W : (b + 1) * W], l, 1, 1)
-
-    def arrive(j):
+    def arrive(j, factored):
         g = max(j - 1, 0)
         for i in range(j + 1):
             f, k = (j, i) if j < 2 else (i // 2, i % 2)
             left[j, i] = fin[g, f, k * ns : (k + 1) * ns].reshape(W, W) * scale
-        basis_ref[:, j * W : (j + 1) * W] = s_ref[:, j * W : (j + 1) * W]
-        arrived.append(j)
-        for b in done:
+        for b in range(factored):
             catch_up(j, b)
-        for b in done:
-            settle(j, b)
+
+    def basis(b):
+        here = slice(b * W, (b + 1) * W)
+        value = s_ref[:, here]
+        for m in range(b):
+            value = value - mm(basis_ref[:, m * W : (m + 1) * W], low[b, m], 1, 1)
+            upper[m, :, here] = low[b, m].T
+        basis_ref[:, here] = value if b == CHUNKS - 1 else mm(value, diag[b], 1, 1)
 
     def factor(b, hooks=None):
         w_ref[...] = left[b, b]
         factor_block(w_ref, q_ref, hooks)
-        q = q_ref[...]
-        diag[b] = q
+        diag[b] = q_ref[...]
         upper[b, :, b * W : (b + 1) * W] = jnp.where(col_at >= row_at, w_ref[...], 0.0)
-        later = [j for j in arrived if j > b]
-        for j in later:
-            catch_up(j, b)
-        block = (slice(None), slice(b * W, (b + 1) * W))
-        basis_ref[block] = mm(basis_ref[block], q, 1, 1)
-        for j in later:
-            settle(j, b)
-        done.append(b)
 
     for j in range(CHUNKS):
         z_send(j)
@@ -380,19 +367,26 @@
     spread(1)
     spread_core(0)
     spread_end(0)
-    spread(2)
-    arrive(0)
-    arrive(1)
-    factor(0)
-    spread_core(1)
-    factor(1)
-    spread_end(1)
-    spread_core(2)
-    arrive(2)
-    factor(2)
-    spread_end(2)
-    arrive(3)
-    factor(3)
+    arrive(0, 0)
+    arrive(1, 0)
+    factor(0, {3: lambda: spread(2), 13: lambda: spread_core(1)})
+    catch_up(1, 0)
+
+    def row_two():
+        spread_end(1)
+        arrive(2, 1)
+
+    def row_three():
+        spread_end(2)
+        arrive(3, 2)
+
+    factor(1, {2: lambda: basis(0), 6: row_two, 12: lambda: spread_core(2)})
+    catch_up(2, 1)
+    factor(2, {2: lambda: basis(1), 6: row_three})
+    catch_up(3, 2)
+    factor(3, {2: lambda: basis(2), 6: lambda: basis(3)})
+    last = slice((CHUNKS - 1) * W, CHUNKS * W)
+    basis_ref[:, last] = mm(basis_ref[:, last], diag[CHUNKS - 1], 1, 1)
     out_ref[...] = upper[x]
 
     for j in range(CHUNKS):

time: 96.8 us -> 90.7 us (0.937)
  Pallas kernels: 92.4 us -> 87.7 us
  local copies, waits for them, and re-layouts: 3.54 us -> 2.21 us
    pallas_call x1, Pallas kernels: 92.4 us -> 87.7 us  [on_device(): pl.pallas_call(functools.partial(sketch_kernel, nz, nx, scale), out_shape...]
    unnamed x2 -> x4, local copies, waits for them, and re-layouts: 3.54 us -> 2.21 us
where the time goes in v6:
time: 90.7 us; the launch traced here: 90.5 us
  Pallas kernels  87.7 us (97%)
  local copies, waits for them, and re-layouts  2.21 us (2%)
    pallas_call x1, Pallas kernels, on_device(): pl.pallas_call(functools.partial(sketch_kernel, nz, nx, scale), out_shape...  87.7 us
    unnamed x4, local copies, waits for them, and re-layouts  2.21 us

profile of v6, /device:TPU:1, one launch (start us, length us, event | category | flops | bytes accessed | tf_op | source)
XLA Modules:
  0.0 90.5 jit_solution(4989316578613446981)
XLA Ops:
  0.6 0.0 copy-start
  0.6 0.7 copy-done
  1.3 87.7 %shard_map.41 = (f32[256,512]{1,0:T(8,128)S(1)}, f32[128,512]{1,0:T(8,128)S(1)}) custom-call(bf16[1024,2048]{1,0:T(8,128)(2,1)} %a_hbm.1, bf16[16,512]{1,0:T(8,128)(2,1)S(1)} %copy-done), custom_call_target="tpu_custom_call" | custom-call | tf_op jit(solution)/shard_map/pallas_call | solution.py:419
  89.0 0.8 copy.6
  89.8 0.7 copy.7
Async XLA Ops:
  0.6 0.7 copy-start
